TPU v7x, 256 devices: a whole 4x4x8 slice. The times are simulated.
256 devices in a mesh: replica: 32 (over x, z), shard: 8 (over y, core).
Axes of the slice: x: 4, y: 4, z: 8, core: 2. Of those that a mesh axis runs over, the one named last changes fastest.
Arguments:
- grads: bfloat16 [32, 8192, 2048], P('replica', 'shard'), may hold values from -64 to 64
- errors: bfloat16 [32, 8192, 2048], P('replica', 'shard'), may hold values from -4 to 4
- q_prev: bfloat16 [32, 2048], P(None, 'shard'), may hold values from -6 to 6
- momentum: float32 [8192, 2048], P('shard', 'replica'), may hold values from -1.2 to 1.2
Outputs:
- new_errors: bfloat16 [32, 8192, 2048], P('replica', 'shard')
- new_momentum: float32 [8192, 2048], P('shard', 'replica')
- q_next: float32 [32, 2048], P(None, 'shard')
All inputs are finite; a program needn't handle non-finite values.
Results may differ from a plain program's by a relative error of at most 0.012.
Values may be sent and summed in bfloat16 or wider, within the bound.
A program may use at most 64 MiB of HBM per device.

v0:
```python
import jax
import jax.numpy as jnp
from jax import lax
from jax.sharding import PartitionSpec as P


def shards(grads, errors, q_prev, momentum):
    highest = lax.Precision.HIGHEST
    merged = grads[0].astype(jnp.float32) + errors[0].astype(jnp.float32)
    col_count = merged.shape[1]
    product = lax.dot_general(
        merged,
        lax.all_gather(q_prev, "shard", axis=1, tiled=True).astype(jnp.float32),
        (((1,), (1,)), ((), ())),
        precision=highest,
    )
    factor = lax.psum(product.astype(jnp.bfloat16), "replica").astype(jnp.float32)
    every_row = lax.all_gather(factor.astype(jnp.bfloat16), "shard", axis=0, tiled=True).astype(
        factor.dtype
    )
    gram_matrix = jnp.dot(every_row.T, every_row, precision=highest)
    lower_factor = jnp.linalg.cholesky(gram_matrix)
    ortho = jax.scipy.linalg.solve_triangular(lower_factor, factor.T, lower=True).T
    right_term = jnp.dot(ortho.T, merged, precision=highest)
    replicas = lax.axis_size("replica")
    block_width = col_count // lax.axis_size("shard")
    right_full = lax.psum(right_term, ("replica", "shard")) / replicas
    q_next = lax.dynamic_slice_in_dim(
        right_full, lax.axis_index("shard") * block_width, block_width, 1
    )
    approx = jnp.dot(ortho, right_full, precision=highest)
    new_errors = (merged - approx).astype(jnp.bfloat16)[None]
    momentum_width = momentum.shape[1]
    approx_block = lax.dynamic_slice_in_dim(
        approx, lax.axis_index("replica") * momentum_width, momentum_width, 1
    )
    new_momentum = 0.9 * momentum + approx_block
    return (new_errors, new_momentum, q_next)


def solution(mesh):
    return jax.shard_map(
        shards,
        mesh=mesh,
        in_specs=(
            P("replica", "shard", None),
            P("replica", "shard", None),
            P(None, "shard"),
            P("shard", "replica"),
        ),
        out_specs=(P("replica", "shard", None), P("shard", "replica"), P(None, "shard")),
        check_vma=False,
    )
```

profile of v0, /device:TPU:1, one launch (start us, length us, event | category | flops | bytes accessed | tf_op | source)
XLA Modules:
  0.0 478.2 jit_solution(6031099820396762904)
XLA Ops:
  7.2 0.0 all-reduce.3.cloned.1.call-start
  7.2 16.1 %all_gather.6 = bf16[32,2048]{1,0:T(8,128)(2,1)S(1)} all-gather(bf16[32,256]{1,0:T(8,128)(2,1)} %param.6), channel_id=1, replica_groups=mesh['replica'=32,'shard'=8] {'shard'}, dimensions={1}, use_global_device_ids=true | all-gather | bytes 147456 | tf_op jit(solution)/shard_map/all_gather | solution.py:13
  23.3 0.0 copy-start.2
  23.3 9.1 %fusion.6 = bf16[1024,32]{0,1:T(8,128)(2,1)} fusion(bf16[32,2048]{1,0:T(8,128)(2,1)S(1)} %all_gather.6, bf16[1,1024,2048]{2,1,0:T(8,128)(2,1)} %param.5, bf16[1,1024,2048]{2,1,0:T(8,128)(2,1)} %param.4), kind=kOutput, calls=%fused_computation.8 | convolution fusion | flops 811630592 | bytes 8585216 | tf_op jit(solution)/shard_map/dot_general | solution.py:11
  32.3 0.0 all-reduce.3.cloned.1.call-update
  32.3 0.0 all-reduce.5.cloned.1.call-start
  32.4 135.6 %all-reduce.3.cloned.1.call-done = bf16[1024,32]{0,1:T(8,128)(2,1)} async-done(((bf16[1024,32]{0,1:T(8,128)(2,1)}), bf16[1024,32]{0,1:T(8,128)(2,1)}) %all-reduce.3.cloned.1.call-update) | async-done | bytes 65552 | tf_op jit(solution)/shard_map/psum | solution.py:17
  168.0 18.3 %all_gather.7 = bf16[8192,32]{0,1:T(8,128)(2,1)S(1)} all-gather(bf16[1024,32]{0,1:T(8,128)(2,1)} %all-reduce.3.cloned.1.call-done), channel_id=1, replica_groups=mesh['replica'=32,'shard'=8] {'shard'}, dimensions={0}, use_global_device_ids=true | all-gather | bytes 589824 | tf_op jit(solution)/shard_map/all_gather | solution.py:18
  186.4 0.3 fusion.14
  186.6 0.1 copy.7
  186.7 2.9 cholesky.16
  189.7 0.6 compare_reduce_fusion
  190.3 0.7 fusion.9
  191.0 2.4 custom-call.7
  193.4 1.1 fusion.10
  194.6 8.6 %fusion = f32[32,2048]{1,0:T(8,128)} fusion(f32[32,1024]{1,0:T(8,128)S(1)} %fusion.10, bf16[1,1024,2048]{2,1,0:T(8,128)(2,1)} %param.5, bf16[1,1024,2048]{2,1,0:T(8,128)(2,1)} %param.4), kind=kOutput, calls=%fused_computation.1 | convolution fusion | flops 811597824 | bytes 8781824 | tf_op jit(solution)/shard_map/dot_general | solution.py:24
  203.1 0.0 all-reduce.5.cloned.1.call-update
  203.1 0.0 copy-done.2
  203.1 0.2 copy.8
  203.3 246.0 %all-reduce.5.cloned.1.call-done = f32[32,2048]{1,0:T(8,128)} async-done(((f32[32,2048]{1,0:T(8,128)}), f32[32,2048]{1,0:T(8,128)}) %all-reduce.5.cloned.1.call-update) | async-done | bytes 262160 | tf_op jit(solution)/shard_map/psum | solution.py:27
  449.4 0.0 copy-start
  449.4 10.0 %fusion.13 = f32[1024,2048]{1,0:T(8,128)} fusion(f32[32,1024]{1,0:T(8,128)S(1)} %fusion.10, f32[32,2048]{1,0:T(8,128)} %all-reduce.5.cloned.1.call-done), kind=kOutput, calls=%fused_computation.22 | convolution fusion | flops 805371904 | bytes 8781824 | tf_op jit(solution)/shard_map/dot_general | solution.py:31
  459.4 0.0 copy-done
  459.4 0.0 copy-start.1
  459.4 9.2 %fusion.5 = bf16[1,1024,2048]{2,1,0:T(8,128)(2,1)} fusion(f32[1024,2048]{1,0:T(8,128)} %fusion.13, bf16[1,1024,2048]{2,1,0:T(8,128)(2,1)S(1)} %copy-done, bf16[1,1024,2048]{2,1,0:T(8,128)(2,1)} %param.4), kind=kLoop, calls=%fused_computation.7 | loop fusion | flops 10485760 | bytes 20971520 | tf_op jit(solution)/shard_map/broadcast_in_dim | solution.py:32
  468.6 1.2 dynamic-slice_add_fusion
  469.8 0.9 copy.9
  470.7 0.0 copy-done.1
  470.8 0.6 constant_dynamic-slice_fusion
  (3 shorter events, 0.1 us)
Async XLA Ops:
  7.2 160.9 %all-reduce.3.cloned.1.call-start = ((), (), s32[]{:S(2)}) async-start(), calls=%async_computation | async-start | bytes 131072 | tf_op jit(solution)/shard_map/psum | solution.py:17
  23.3 179.9 %copy-start.2 = (f32[1024,64]{0,1:T(8,128)S(1)}, f32[1024,64]{0,1:T(8,128)}, u32[]{:S(2)}) copy-start(f32[1024,64]{0,1:T(8,128)} %param.7) | copy-start | bytes 786436
  32.3 417.0 %all-reduce.5.cloned.1.call-start = ((), (), s32[]{:S(2)}) async-start(), calls=%async_computation.1 | async-start | bytes 524288 | tf_op jit(solution)/shard_map/psum | solution.py:27
  449.4 10.0 %copy-start = (bf16[1,1024,2048]{2,1,0:T(8,128)(2,1)S(1)}, bf16[1,1024,2048]{2,1,0:T(8,128)(2,1)}, u32[]{:S(2)}) copy-start(bf16[1,1024,2048]{2,1,0:T(8,128)(2,1)} %param.5) | copy-start | bytes 12582916
  459.4 11.4 %copy-start.1 = (f32[32,2048]{1,0:T(8,128)S(1)}, f32[32,2048]{1,0:T(8,128)}, u32[]{:S(2)}) copy-start(f32[32,2048]{1,0:T(8,128)} %all-reduce.5.cloned.1.call-done) | copy-start | bytes 786436
Sparse Core Ops, SparseCore 0:
  32.5 135.5 all-reduce.2
  203.2 246.0 all-reduce.4
where the time goes:
time: 479 us; the launch traced here: 478 us
  waiting for transfers between devices  382 us (80%)
  blocking collectives  34.4 us (7%)
  matrix products  29 us (6%)
  other arithmetic  17.2 us (4%)
  between operations  14.1 us (3%)
    psum x1, waiting for transfers between devices, shards(): right_full = lax.psum(right_term, ('replica', 'shard')) / replicas  246 us
    psum x1, waiting for transfers between devices, shards(): lax.psum(product.astype(jnp.bfloat16), 'replica').astype(jnp.float32)  136 us
    all_gather x1, blocking collectives, shards(): lax.all_gather(factor.astype(jnp.bfloat16), 'shard', axis=0, tiled=True)  18.3 us
    all_gather x1, blocking collectives, shards(): lax.all_gather(q_prev, 'shard', axis=1, tiled=True).astype(jnp.float32)  16.1 us
    dot_general x1, matrix products, shards(): approx = jnp.dot(ortho, right_full, precision=highest)  9.98 us
  transfers between devices with their start and end apart: 2, of which 2 were waited for; matrix products, arithmetic and copies ran while one was open for 0% of the time, Pallas kernels for 0%

commit v1 on v0

v1 whole, which is shorter than its diff:
```python
import functools

import jax
import jax.numpy as jnp
from jax import lax
from jax.experimental import pallas as pl
from jax.experimental.pallas import tpu as pltpu
from jax.sharding import PartitionSpec as P

MESH = pl.DeviceIdType.MESH
NX, NZ, NS = 4, 8, 8
NM = NX * NS
ROWS, COLS, R = 1024, 2048, 32
CH = ROWS // NX
F32, BF16 = jnp.float32, jnp.bfloat16
HIGHEST = lax.Precision.HIGHEST


def dot(a, b, dims, precision=None):
    return lax.dot_general(
        a, b, (dims, ((), ())), precision=precision, preferred_element_type=F32
    )


def wait_bytes(ref, sem):
    pltpu.make_async_copy(ref, ref, sem).wait()


def inverse_factor(gram):
    row = lax.broadcasted_iota(jnp.int32, (R, 128), 0)
    lane = lax.broadcasted_iota(jnp.int32, (R, 128), 1)
    eye = jnp.where(row == lane, 1.0, 0.0).astype(F32)
    work = eye + jnp.concatenate(
        [jnp.zeros((R, R), F32), gram, jnp.zeros((R, 128 - 2 * R), F32)], axis=1
    )
    pivots = jnp.ones((R, 128), F32)
    for j in range(R):
        column = jnp.broadcast_to(work[:, R + j : R + j + 1], (R, 128))
        pivot = column[j : j + 1, :]
        pivots = jnp.where(row == j, pivot, pivots)
        scaled = work[j : j + 1, :] * (1.0 / pivot)
        work = work - jnp.where(row > j, column, 0.0) * scaled
    return work[:, :R] * lax.rsqrt(pivots)[:, :R]


def exchange_kernel(
    g_hbm,
    e_hbm,
    q_ref,
    ohl_ref,
    qn_ref,
    qsel_ref,
    gv,
    ev,
    qb,
    xs,
    xr,
    zb,
    pt,
    gb,
    st,
    rt,
    tz,
    qp,
    load_sem,
    send_sem,
    recv_sem,
):
    replica = lax.axis_index("replica")
    s = lax.axis_index("shard")
    x, z = replica // NZ, lax.rem(replica, NZ)
    m = x * NS + s

    def shard_peer(i):
        return (replica, lax.rem(s + i, NS))

    def x_peer(i):
        return (lax.rem(x + i, NX) * NZ + z, s)

    def z_peer(i):
        return (x * NZ + lax.rem(z + i, NZ), s)

    def m_device(p):
        return ((p // NS) * NZ + z, lax.rem(p, NS))

    def send(src, dst, at, device):
        pltpu.make_async_remote_copy(
            src,
            dst,
            send_sem.at[at],
            recv_sem.at[at],
            device_id=device,
            device_id_type=MESH,
        ).start()

    loads = []
    for i in range(1, NX + 1):
        rows = pl.ds(pl.multiple_of(lax.rem(x + i, NX) * CH, CH), CH)
        pair = [
            pltpu.make_async_copy(src.at[rows], dst.at[rows], load_sem.at[2 * (i - 1) + k])
            for k, (src, dst) in enumerate(((g_hbm, gv), (e_hbm, ev)))
        ]
        for copy in pair:
            copy.start()
        loads.append(pair)

    barrier = pltpu.get_barrier_semaphore()

    def greet(i, carry):
        pl.semaphore_signal(
            barrier, inc=1, device_id=m_device(lax.rem(m + i, NM)), device_id_type=MESH
        )
        return carry

    lax.fori_loop(1, NM, greet, 0)
    for i in range(1, NZ):
        pl.semaphore_signal(barrier, inc=1, device_id=z_peer(i), device_id_type=MESH)
    pl.semaphore_wait(barrier, NM - 1 + NZ - 1)

    for i in range(1, NS):
        send(q_ref, qb.at[s], 0, shard_peer(i))
    qb[s] = q_ref[...]
    wait_bytes(qb.at[pl.ds(0, NS - 1)], recv_sem.at[0])

    own = None
    for i in range(1, NX + 1):
        chunk = lax.rem(x + i, NX)
        rows = pl.ds(pl.multiple_of(chunk * CH, CH), CH)
        for copy in loads[i - 1]:
            copy.wait()
        total = jnp.zeros((R, CH), F32)
        for k in range(NS):
            columns = pl.ds(k * 256, 256)
            total += dot(qb[k], gv[rows, columns], ((1,), (1,)))
            total += dot(qb[k], ev[rows, columns], ((1,), (1,)))
        if i < NX:
            xs[i - 1] = total.astype(BF16)
            send(xs.at[i - 1], xr.at[x], 1, x_peer(i))
        else:
            xr[x] = total.astype(BF16)
    wait_bytes(xr.at[pl.ds(0, NX - 1)], recv_sem.at[1])
    total = xr[0].astype(F32)
    for k in range(1, NX):
        total += xr[k].astype(F32)
    zb[z] = total.astype(BF16)
    for i in range(1, NZ):
        send(zb.at[z], zb.at[z], 2, z_peer(i))
    wait_bytes(zb.at[pl.ds(0, NZ - 1)], recv_sem.at[2])
    total = zb[0].astype(F32)
    for k in range(1, NZ):
        total += zb[k].astype(F32)
    pt[x] = total.astype(BF16)
    for i in range(1, NX):
        send(pt.at[x], pt.at[x], 3, x_peer(i))
    wait_bytes(pt.at[pl.ds(0, NX - 1)], recv_sem.at[3])

    gram = jnp.zeros((R, R), F32)
    for c in range(NX):
        gram += dot(pt[c], pt[c], ((1,), (1,)))
    gb[s] = jnp.concatenate([gram[8 * k : 8 * k + 8] for k in range(4)], axis=1)
    for i in range(1, NS):
        send(gb.at[s], gb.at[s], 4, shard_peer(i))

    low = lax.broadcasted_iota(jnp.int32, (16, 128), 1) < 64

    def right_block(i, carry):
        block = lax.rem(m // 4 + i, 8)
        columns = pl.ds(pl.multiple_of(block * 256, 256), 256)
        term = jnp.zeros((R, 256), F32)
        for c in range(NX):
            rows = pl.ds(c * CH, CH)
            term += dot(pt[c], gv[rows, columns], ((1,), (0,)))
            term += dot(pt[c], ev[rows, columns], ((1,), (0,)))
        for t in range(2):
            top = term[:16, 128 * t : 128 * t + 128]
            bottom = term[16:, 128 * t : 128 * t + 128]
            for h in range(2):
                p = block * 4 + 2 * t + h
                if h == 0:
                    piece = jnp.where(low, top, pltpu.roll(bottom, 64, 1))
                else:
                    piece = jnp.where(low, pltpu.roll(top, 64, 1), bottom)
                st[p] = piece

                @pl.when(p != m)
                def _():
                    send(st.at[p], rt.at[m], 5, m_device(p))

        return carry

    lax.fori_loop(1, 9, right_block, 0)
    rt[m] = st[m]

    wait_bytes(gb.at[pl.ds(0, NS - 1)], recv_sem.at[4])
    packed = gb[0]
    for k in range(1, NS):
        packed += gb[k]
    gram = jnp.concatenate([packed[:, R * k : R * k + R] for k in range(4)], axis=0)
    inverse = inverse_factor(gram)

    wait_bytes(rt.at[pl.ds(0, NM - 1)], recv_sem.at[5])
    piece = rt[0]
    for k in range(1, NM):
        piece += rt[k]
    tz[z] = piece
    for i in range(1, NZ):
        send(tz.at[z], tz.at[z], 6, z_peer(i))

    for c in range(NX):
        ortho = dot(pt[c].astype(F32), inverse, ((0,), (1,)), HIGHEST)
        high = ortho.astype(BF16)
        rest = (ortho - high.astype(F32)).astype(BF16)
        ohl_ref[pl.ds(c * CH, CH), :] = jnp.concatenate([high, rest], axis=1)

    wait_bytes(tz.at[pl.ds(0, NZ - 1)], recv_sem.at[6])
    piece = tz[0]
    for k in range(1, NZ):
        piece += tz[k]
    term = jnp.concatenate([piece, pltpu.roll(piece, 64, 1)], axis=0)
    right = dot(inverse, term, ((1,), (0,)), HIGHEST) * (1.0 / 32.0)
    qp[m] = jnp.where(low, right[:16], pltpu.roll(right[16:], 64, 1)).astype(BF16)

    def gather(i, carry):
        send(qp.at[m], qp.at[m], 7, m_device(lax.rem(m + i, NM)))
        return carry

    lax.fori_loop(1, NM, gather, 0)
    wait_bytes(qp.at[pl.ds(0, NM - 1)], recv_sem.at[7])
    for t in range(NM // 2):
        first, second = qp[2 * t].astype(F32), qp[2 * t + 1].astype(F32)
        columns = pl.ds(128 * t, 128)
        qn_ref[:16, columns] = jnp.where(low, first, pltpu.roll(second, 64, 1)).astype(BF16)
        qn_ref[16:, columns] = jnp.where(low, pltpu.roll(first, 64, 1), second).astype(BF16)
    mine = qp[replica].astype(F32)
    qsel_ref[:16] = mine.astype(BF16)
    qsel_ref[16:] = pltpu.roll(mine, 64, 1).astype(BF16)

    for ref, at in (
        (qb.at[pl.ds(0, NS - 1)], 0),
        (xr.at[pl.ds(0, NX - 1)], 1),
        (zb.at[pl.ds(0, NZ - 1)], 2),
        (pt.at[pl.ds(0, NX - 1)], 3),
        (gb.at[pl.ds(0, NS - 1)], 4),
        (rt.at[pl.ds(0, NM - 1)], 5),
        (tz.at[pl.ds(0, NZ - 1)], 6),
        (qp.at[pl.ds(0, NM - 1)], 7),
    ):
        wait_bytes(ref, send_sem.at[at])


def residual_kernel(g_ref, e_ref, ohl_ref, qn_ref, qsel_ref, mom_ref, err_ref, new_ref, q_ref):
    s = lax.axis_index("shard")
    q = qn_ref[...]
    ohl = ohl_ref[...]
    approx = dot(ohl, jnp.concatenate([q, q], axis=0), ((1,), (0,)))
    merged = g_ref[...].astype(F32) + e_ref[...].astype(F32)
    err_ref[...] = (merged - approx).astype(BF16)
    chosen = qsel_ref[...]
    block = dot(ohl, jnp.concatenate([chosen, chosen], axis=0), ((1,), (0,)))
    new_ref[...] = 0.9 * mom_ref[...] + block[:, :64]
    q_ref[...] = qn_ref[:, pl.ds(pl.multiple_of(s * 256, 256), 256)].astype(F32)


def shards(grads, errors, q_prev, momentum):
    g, e = grads[0], errors[0]
    vmem = pl.BlockSpec(memory_space=pltpu.VMEM)
    hbm = pl.BlockSpec(memory_space=pltpu.HBM)
    ohl, qn, qsel = pl.pallas_call(
        exchange_kernel,
        out_shape=(
            jax.ShapeDtypeStruct((ROWS, 2 * R), BF16),
            jax.ShapeDtypeStruct((R, COLS), BF16),
            jax.ShapeDtypeStruct((R, 128), BF16),
        ),
        in_specs=[hbm, hbm, vmem],
        out_specs=(vmem, vmem, vmem),
        scratch_shapes=[
            pltpu.VMEM((ROWS, COLS), BF16),
            pltpu.VMEM((ROWS, COLS), BF16),
            pltpu.VMEM((NS, R, 256), BF16),
            pltpu.VMEM((NX - 1, R, CH), BF16),
            pltpu.VMEM((NX, R, CH), BF16),
            pltpu.VMEM((NZ, R, CH), BF16),
            pltpu.VMEM((NX, R, CH), BF16),
            pltpu.VMEM((NS, 8, 128), F32),
            pltpu.VMEM((NM, 16, 128), F32),
            pltpu.VMEM((NM, 16, 128), F32),
            pltpu.VMEM((NZ, 16, 128), F32),
            pltpu.VMEM((NM, 16, 128), BF16),
            pltpu.SemaphoreType.DMA((2 * NX,)),
            pltpu.SemaphoreType.DMA((8,)),
            pltpu.SemaphoreType.DMA((8,)),
        ],
        compiler_params=pltpu.CompilerParams(
            collective_id=0, has_side_effects=True, vmem_limit_bytes=40 << 20
        ),
    )(g, e, q_prev)
    tile = 128
    new_errors, new_momentum, q_next = pl.pallas_call(
        residual_kernel,
        grid=(ROWS // tile,),
        out_shape=(
            jax.ShapeDtypeStruct((ROWS, COLS), BF16),
            jax.ShapeDtypeStruct((ROWS, 64), F32),
            jax.ShapeDtypeStruct((R, 256), F32),
        ),
        in_specs=[
            pl.BlockSpec((tile, COLS), lambda i: (i, 0)),
            pl.BlockSpec((tile, COLS), lambda i: (i, 0)),
            pl.BlockSpec((tile, 2 * R), lambda i: (i, 0)),
            pl.BlockSpec((R, COLS), lambda i: (0, 0)),
            pl.BlockSpec((R, 128), lambda i: (0, 0)),
            pl.BlockSpec((tile, 64), lambda i: (i, 0)),
        ],
        out_specs=(
            pl.BlockSpec((tile, COLS), lambda i: (i, 0)),
            pl.BlockSpec((tile, 64), lambda i: (i, 0)),
            pl.BlockSpec((R, 256), lambda i: (0, 0)),
        ),
        compiler_params=pltpu.CompilerParams(vmem_limit_bytes=40 << 20),
    )(g, e, ohl, qn, qsel, momentum)
    return (new_errors[None], new_momentum, q_next)


def solution(mesh):
    return jax.shard_map(
        shards,
        mesh=mesh,
        in_specs=(
            P("replica", "shard", None),
            P("replica", "shard", None),
            P(None, "shard"),
            P("shard", "replica"),
        ),
        out_specs=(P("replica", "shard", None), P("shard", "replica"), P(None, "shard")),
        check_vma=False,
    )
```

time: 479 us -> 66.1 us (0.14)
  waiting for transfers between devices: 382 us -> 0 us
  Pallas kernels: 0 us -> 54.6 us
  blocking collectives: 34.4 us -> 0 us
  matrix products: 29 us -> 0 us
  other arithmetic: 17.2 us -> 0 us
  between operations: 14.1 us -> 0.68 us
  local copies, waits for them, and re-layouts: 1.8 us -> 10.5 us
    psum x2 -> x0, waiting for transfers between devices: 382 us -> none  [the longest x1 246 us: shards(): right_full = lax.psum(right_term, ('replica', 'shard')) / replicas]
    pallas_call x0 -> x2, Pallas kernels: none -> 54.6 us  [the longest x1 49.9 us: shards(): pl.pallas_call(exchange_kernel, out_shape=(jax.ShapeDtypeStruct((ROWS, 2...]
    all_gather x2 -> x0, blocking collectives: 34.4 us -> none  [the longest x1 18.3 us: shards(): lax.all_gather(factor.astype(jnp.bfloat16), 'shard', axis=0, tiled=True)]
    dot_general x4 -> x0, matrix products: 27.8 us -> none  [the longest x1 9.98 us: shards(): approx = jnp.dot(ortho, right_full, precision=highest)]
    unnamed x8 -> x14, local copies, waits for them, and re-layouts: 1.09 us -> 10.5 us
    broadcast_in_dim x1 -> x0, other arithmetic: 9.22 us -> none  [shards(): new_errors = (merged - approx).astype(jnp.bfloat16)[None]]
    another operation x5 -> x0, other arithmetic: 6.69 us -> none  [the longest x3 3.6 us: shards(): lower_factor = jnp.linalg.cholesky(gram_matrix)]
  transfers between devices with their start and end apart: 2 -> 0, of which waited for: 2 -> 0; matrix products, arithmetic and copies ran while one was open for 0% -> 0% of each run, Pallas kernels for 0% -> 0%
where the time goes in v1:
time: 66.1 us; the launch traced here: 65.8 us
  Pallas kernels  54.6 us (83%)
  local copies, waits for them, and re-layouts  10.5 us (16%)
  between operations  0.68 us (1%)
    pallas_call x1, Pallas kernels, shards(): pl.pallas_call(exchange_kernel, out_shape=(jax.ShapeDtypeStruct((ROWS, 2...  49.9 us
    unnamed x14, local copies, waits for them, and re-layouts  10.5 us
    pallas_call x1, Pallas kernels, shards(): pl.pallas_call(residual_kernel, grid=(ROWS // tile,), out_shape=(jax.Shap...  4.63 us

profile of v1, /device:TPU:1, one launch (start us, length us, event | category | flops | bytes accessed | tf_op | source)
XLA Modules:
  0.0 65.8 jit_solution(6832399492847585951)
XLA Ops:
  0.6 0.0 copy-start
  0.6 2.2 %copy-done = bf16[1,1024,2048]{2,1,0:T(8,128)(2,1)S(1)} copy-done((bf16[1,1024,2048]{2,1,0:T(8,128)(2,1)S(1)}, bf16[1,1024,2048]{2,1,0:T(8,128)(2,1)}, u32[]{:S(2)}) %copy-start) | copy-done | bytes 4194328
  2.8 0.0 copy-start.2
  2.8 2.2 %copy-done.2 = bf16[1,1024,2048]{2,1,0:T(8,128)(2,1)S(1)} copy-done((bf16[1,1024,2048]{2,1,0:T(8,128)(2,1)S(1)}, bf16[1,1024,2048]{2,1,0:T(8,128)(2,1)}, u32[]{:S(2)}) %copy-start.2) | copy-done | bytes 4194328
  5.0 0.0 copy-start.4
  5.0 0.7 %copy-done.4 = bf16[32,256]{1,0:T(8,128)(2,1)S(1)} copy-done((bf16[32,256]{1,0:T(8,128)(2,1)S(1)}, bf16[32,256]{1,0:T(8,128)(2,1)}, u32[]{:S(2)}) %copy-start.4) | copy-done | bytes 16408
  5.7 0.0 copy-start.5
  5.7 49.9 %shard_map.67 = (bf16[1024,64]{1,0:T(8,128)(2,1)S(1)}, bf16[32,2048]{1,0:T(8,128)(2,1)S(1)}, bf16[32,128]{1,0:T(8,128)(2,1)S(1)}) custom-call(bf16[1024,2048]{1,0:T(8,128)(2,1)S(1)} %bitcast.3, bf16[1024,2048]{1,0:T(8,128)(2,1)S(1)} %bitcast.5, bf16[32,256]{1,0:T(8,128)(2,1)S(1)} %copy-done.4), custom_call_target="tpu_custom_call" | custom-call | tf_op jit(solution)/shard_map/pallas_call | solution.py:268
  55.7 0.0 copy-done.5
  55.7 0.2 copy.7.mom_ref
  55.9 0.0 copy-start.1
  55.9 2.2 %copy-done.1 = bf16[1,1024,2048]{2,1,0:T(8,128)(2,1)S(1)} copy-done((bf16[1,1024,2048]{2,1,0:T(8,128)(2,1)S(1)}, bf16[1,1024,2048]{2,1,0:T(8,128)(2,1)}, u32[]{:S(2)}) %copy-start.1) | copy-done | bytes 4194328
  58.1 0.0 copy-start.3
  58.1 2.2 %copy-done.3 = bf16[1,1024,2048]{2,1,0:T(8,128)(2,1)S(1)} copy-done((bf16[1,1024,2048]{2,1,0:T(8,128)(2,1)S(1)}, bf16[1,1024,2048]{2,1,0:T(8,128)(2,1)}, u32[]{:S(2)}) %copy-start.3) | copy-done | bytes 4194328
  60.3 4.6 %shard_map.68 = (bf16[1024,2048]{1,0:T(8,128)(2,1)}, f32[1024,64]{1,0:T(8,128)S(1)}, f32[32,256]{1,0:T(8,128)}) custom-call(bf16[1024,2048]{1,0:T(8,128)(2,1)S(1)} %bitcast.4, bf16[1024,2048]{1,0:T(8,128)(2,1)S(1)} %bitcast.6, bf16[1024,64]{1,0:T(8,128)(2,1)S(1)} %get-tuple-element.9.ohl_ref, bf16[32,2048]{1,0:T(8,128)(2,1)S(1)} %get-tuple-element.10.qn_ref, ...), custom_call_target="tpu_custom_call" | custom-call | tf_op jit(solution)/shard_map/pallas_call | solution.py:299
  64.9 0.9 %copy.8 = f32[1024,64]{0,1:T(8,128)} copy(f32[1024,64]{1,0:T(8,128)S(1)} %get-tuple-element.16) | data formatting | bytes 524288
Async XLA Ops:
  0.6 2.2 %copy-start = (bf16[1,1024,2048]{2,1,0:T(8,128)(2,1)S(1)}, bf16[1,1024,2048]{2,1,0:T(8,128)(2,1)}, u32[]{:S(2)}) copy-start(bf16[1,1024,2048]{2,1,0:T(8,128)(2,1)} %param.4) | copy-start | bytes 12582916
  2.8 2.2 %copy-start.2 = (bf16[1,1024,2048]{2,1,0:T(8,128)(2,1)S(1)}, bf16[1,1024,2048]{2,1,0:T(8,128)(2,1)}, u32[]{:S(2)}) copy-start(bf16[1,1024,2048]{2,1,0:T(8,128)(2,1)} %param.5) | copy-start | bytes 12582916
  5.0 0.7 %copy-start.4 = (bf16[32,256]{1,0:T(8,128)(2,1)S(1)}, bf16[32,256]{1,0:T(8,128)(2,1)}, u32[]{:S(2)}) copy-start(bf16[32,256]{1,0:T(8,128)(2,1)} %q_ref.1) | copy-start | bytes 49156
  5.7 49.9 %copy-start.5 = (f32[1024,64]{0,1:T(8,128)S(1)}, f32[1024,64]{0,1:T(8,128)}, u32[]{:S(2)}) copy-start(f32[1024,64]{0,1:T(8,128)} %param.7) | copy-start | bytes 786436
  55.9 2.2 %copy-start.1 = (bf16[1,1024,2048]{2,1,0:T(8,128)(2,1)S(1)}, bf16[1,1024,2048]{2,1,0:T(8,128)(2,1)}, u32[]{:S(2)}) copy-start(bf16[1,1024,2048]{2,1,0:T(8,128)(2,1)} %param.4) | copy-start | bytes 12582916
  58.1 2.2 %copy-start.3 = (bf16[1,1024,2048]{2,1,0:T(8,128)(2,1)S(1)}, bf16[1,1024,2048]{2,1,0:T(8,128)(2,1)}, u32[]{:S(2)}) copy-start(bf16[1,1024,2048]{2,1,0:T(8,128)(2,1)} %param.5) | copy-start | bytes 12582916

commit v2 on v1

--- a/solution.py
+++ b/solution.py
@@ -13,6 +13,7 @@
 ROWS, COLS, R = 1024, 2048, 32
 CH = ROWS // NX
 F32, BF16 = jnp.float32, jnp.bfloat16
+TILE = 128
 HIGHEST = lax.Precision.HIGHEST
 
 
@@ -46,7 +47,8 @@
 def exchange_kernel(
     g_hbm,
     e_hbm,
-    q_ref,
+    q_hbm,
+    merged_ref,
     ohl_ref,
     qn_ref,
     qsel_ref,
@@ -93,6 +95,8 @@
             device_id_type=MESH,
         ).start()
 
+    q_load = pltpu.make_async_copy(q_hbm, qb.at[s], load_sem.at[2 * NX])
+    q_load.start()
     loads = []
     for i in range(1, NX + 1):
         rows = pl.ds(pl.multiple_of(lax.rem(x + i, NX) * CH, CH), CH)
@@ -117,9 +121,9 @@
         pl.semaphore_signal(barrier, inc=1, device_id=z_peer(i), device_id_type=MESH)
     pl.semaphore_wait(barrier, NM - 1 + NZ - 1)
 
+    q_load.wait()
     for i in range(1, NS):
-        send(q_ref, qb.at[s], 0, shard_peer(i))
-    qb[s] = q_ref[...]
+        send(qb.at[s], qb.at[s], 0, shard_peer(i))
     wait_bytes(qb.at[pl.ds(0, NS - 1)], recv_sem.at[0])
 
     own = None
@@ -225,6 +229,13 @@
         return carry
 
     lax.fori_loop(1, NM, gather, 0)
+
+    def merge(i, carry):
+        rows = pl.ds(pl.multiple_of(i * 16, 16), 16)
+        merged_ref[rows, :] = gv[rows, :].astype(F32) + ev[rows, :].astype(F32)
+        return carry
+
+    lax.fori_loop(0, ROWS // 16, merge, 0)
     wait_bytes(qp.at[pl.ds(0, NM - 1)], recv_sem.at[7])
     for t in range(NM // 2):
         first, second = qp[2 * t].astype(F32), qp[2 * t + 1].astype(F32)
@@ -248,32 +259,42 @@
         wait_bytes(ref, send_sem.at[at])
 
 
-def residual_kernel(g_ref, e_ref, ohl_ref, qn_ref, qsel_ref, mom_ref, err_ref, new_ref, q_ref):
+def residual_kernel(
+    merged_ref, ohl_ref, qn_ref, qsel_ref, mom_ref, err_hbm, new_ref, q_ref, staged, sem
+):
     s = lax.axis_index("shard")
     q = qn_ref[...]
-    ohl = ohl_ref[...]
-    approx = dot(ohl, jnp.concatenate([q, q], axis=0), ((1,), (0,)))
-    merged = g_ref[...].astype(F32) + e_ref[...].astype(F32)
-    err_ref[...] = (merged - approx).astype(BF16)
+    q = jnp.concatenate([q, q], axis=0)
+    copies = []
+    for i in range(ROWS // TILE):
+        rows = pl.ds(i * TILE, TILE)
+        approx = dot(ohl_ref[rows, :], q, ((1,), (0,)))
+        staged[rows, :] = (merged_ref[rows, :] - approx).astype(BF16)
+        copies.append(pltpu.make_async_copy(staged.at[rows], err_hbm.at[rows], sem.at[i]))
+        copies[-1].start()
     chosen = qsel_ref[...]
-    block = dot(ohl, jnp.concatenate([chosen, chosen], axis=0), ((1,), (0,)))
-    new_ref[...] = 0.9 * mom_ref[...] + block[:, :64]
+    block = dot(jnp.concatenate([chosen, chosen], axis=0), ohl_ref[...], ((0,), (1,)))
+    new_ref[...] = 0.9 * mom_ref[...] + block[:64]
     q_ref[...] = qn_ref[:, pl.ds(pl.multiple_of(s * 256, 256), 256)].astype(F32)
+    for copy in copies:
+        copy.wait()
 
 
 def shards(grads, errors, q_prev, momentum):
-    g, e = grads[0], errors[0]
+    g = pltpu.with_memory_space_constraint(grads[0], pltpu.HBM)
+    e = pltpu.with_memory_space_constraint(errors[0], pltpu.HBM)
     vmem = pl.BlockSpec(memory_space=pltpu.VMEM)
     hbm = pl.BlockSpec(memory_space=pltpu.HBM)
-    ohl, qn, qsel = pl.pallas_call(
+    merged, ohl, qn, qsel = pl.pallas_call(
         exchange_kernel,
         out_shape=(
+            pltpu.VMEM((ROWS, COLS), F32),
             jax.ShapeDtypeStruct((ROWS, 2 * R), BF16),
             jax.ShapeDtypeStruct((R, COLS), BF16),
             jax.ShapeDtypeStruct((R, 128), BF16),
         ),
-        in_specs=[hbm, hbm, vmem],
-        out_specs=(vmem, vmem, vmem),
+        in_specs=[hbm, hbm, hbm],
+        out_specs=(vmem, vmem, vmem, vmem),
         scratch_shapes=[
             pltpu.VMEM((ROWS, COLS), BF16),
             pltpu.VMEM((ROWS, COLS), BF16),
@@ -287,39 +308,30 @@
             pltpu.VMEM((NM, 16, 128), F32),
             pltpu.VMEM((NZ, 16, 128), F32),
             pltpu.VMEM((NM, 16, 128), BF16),
-            pltpu.SemaphoreType.DMA((2 * NX,)),
+            pltpu.SemaphoreType.DMA((2 * NX + 1,)),
             pltpu.SemaphoreType.DMA((8,)),
             pltpu.SemaphoreType.DMA((8,)),
         ],
         compiler_params=pltpu.CompilerParams(
             collective_id=0, has_side_effects=True, vmem_limit_bytes=40 << 20
         ),
-    )(g, e, q_prev)
-    tile = 128
+    )(g, e, pltpu.with_memory_space_constraint(q_prev, pltpu.HBM))
     new_errors, new_momentum, q_next = pl.pallas_call(
         residual_kernel,
-        grid=(ROWS // tile,),
         out_shape=(
             jax.ShapeDtypeStruct((ROWS, COLS), BF16),
-            jax.ShapeDtypeStruct((ROWS, 64), F32),
+            jax.ShapeDtypeStruct((64, ROWS), F32),
             jax.ShapeDtypeStruct((R, 256), F32),
         ),
-        in_specs=[
-            pl.BlockSpec((tile, COLS), lambda i: (i, 0)),
-            pl.BlockSpec((tile, COLS), lambda i: (i, 0)),
-            pl.BlockSpec((tile, 2 * R), lambda i: (i, 0)),
-            pl.BlockSpec((R, COLS), lambda i: (0, 0)),
-            pl.BlockSpec((R, 128), lambda i: (0, 0)),
-            pl.BlockSpec((tile, 64), lambda i: (i, 0)),
+        in_specs=[vmem] * 5,
+        out_specs=(hbm, vmem, vmem),
+        scratch_shapes=[
+            pltpu.VMEM((ROWS, COLS), BF16),
+            pltpu.SemaphoreType.DMA((ROWS // TILE,)),
         ],
-        out_specs=(
-            pl.BlockSpec((tile, COLS), lambda i: (i, 0)),
-            pl.BlockSpec((tile, 64), lambda i: (i, 0)),
-            pl.BlockSpec((R, 256), lambda i: (0, 0)),
-        ),
         compiler_params=pltpu.CompilerParams(vmem_limit_bytes=40 << 20),
-    )(g, e, ohl, qn, qsel, momentum)
-    return (new_errors[None], new_momentum, q_next)
+    )(merged, ohl, qn, qsel, momentum.T)
+    return (new_errors[None], new_momentum.T, q_next)
 
 
 def solution(mesh):

time: 66.1 us -> 53.3 us (0.81)
  local copies, waits for them, and re-layouts: 10.5 us -> 0.01 us
  Pallas kernels: 54.6 us -> 52.6 us
    unnamed x14 -> x2, local copies, waits for them, and re-layouts: 10.5 us -> 0.01 us
    pallas_call x2, Pallas kernels: 54.6 us -> 52.6 us  [the longest x1 49.5 us: shards(): pl.pallas_call(exchange_kernel, out_shape=(pltpu.VMEM((ROWS, COLS), F32),...]
where the time goes in v2:
time: 53.3 us
  Pallas kernels  52.6 us (99%)
  between operations  0.65 us (1%)
    pallas_call x1, Pallas kernels, shards(): pl.pallas_call(exchange_kernel, out_shape=(pltpu.VMEM((ROWS, COLS), F32),...  49.5 us
    pallas_call x1, Pallas kernels, shards(): pl.pallas_call(residual_kernel, out_shape=(jax.ShapeDtypeStruct((ROWS, CO...  3.05 us

profile of v2, /device:TPU:1, one launch (start us, length us, event | category | flops | bytes accessed | tf_op | source)
XLA Modules:
  0.0 53.3 jit_solution(1225968981829156636)
XLA Ops:
  0.6 0.0 copy-start
  0.6 49.5 %shard_map.67 = (f32[1024,2048]{1,0:T(8,128)S(1)}, bf16[1024,64]{1,0:T(8,128)(2,1)S(1)}, bf16[32,2048]{1,0:T(8,128)(2,1)S(1)}, bf16[32,128]{1,0:T(8,128)(2,1)S(1)}) custom-call(bf16[1024,2048]{1,0:T(8,128)(2,1)} %bitcast.6, bf16[1024,2048]{1,0:T(8,128)(2,1)} %bitcast.7, bf16[32,256]{1,0:T(8,128)(2,1)} %q_hbm.1), custom_call_target="tpu_custom_call" | custom-call | tf_op jit(solution)/shard_map/pallas_call | solution.py:288
  50.2 0.0 copy-done
  50.2 3.1 %shard_map.68 = (bf16[1024,2048]{1,0:T(8,128)(2,1)}, f32[64,1024]{1,0:T(8,128)}, f32[32,256]{1,0:T(8,128)}) custom-call(f32[1024,2048]{1,0:T(8,128)S(1)} %get-tuple-element.10.merged_ref, bf16[1024,64]{1,0:T(8,128)(2,1)S(1)} %get-tuple-element.11.ohl_ref, bf16[32,2048]{1,0:T(8,128)(2,1)S(1)} %get-tuple-element.12.qn_ref, ...), custom_call_target="tpu_custom_call" | custom-call | tf_op jit(solution)/shard_map/pallas_call | solution.py:319
Async XLA Ops:
  0.6 49.6 %copy-start = (f32[1024,64]{0,1:T(8,128)S(1)}, f32[1024,64]{0,1:T(8,128)}, u32[]{:S(2)}) copy-start(f32[1024,64]{0,1:T(8,128)} %param.7) | copy-start | bytes 786436
